TPU v7x, 32 devices: a whole 2x2x4 slice. The times are simulated.
32 devices in a mesh: rows: 16 (over z, y, x), cent: 2 (over core).
Axes of the slice: x: 2, y: 2, z: 4, core: 2. Of those that a mesh axis runs over, the one named last changes fastest.
Arguments:
- passages: bfloat16 [65536, 768], P('rows'), may hold values from -8 to 8
- centroids: bfloat16 [8192, 768], P('cent'), may hold values from -8 to 8
Outputs:
- new_centroids: float32 [8192, 768], P('cent')
- log_row_scale: float32 [65536], P('rows')
All inputs are finite; a program needn't handle non-finite values.
Results may differ from a plain program's by a relative error of at most 0.0042.
Values sent between devices are 32-bit elements; how exact they have to be, the bound alone decides.
A program may use at most 192 MiB of HBM per device.

v0:
```python
import jax
import jax.numpy as jnp
from jax import lax
from jax.sharding import PartitionSpec as P

ITERS = 3


def unit_scale(values):
    full = values.astype(jnp.float32)
    return full * lax.rsqrt(jnp.mean(full * full, axis=-1, keepdims=True) + 1e-06)


def shards(passages, centroids):
    unit_rows = unit_scale(passages).astype(jnp.bfloat16)
    unit_cents = unit_scale(centroids).astype(jnp.bfloat16)
    width = passages.shape[1]
    cosine = jnp.dot(unit_rows, unit_cents.T, preferred_element_type=jnp.float32) / width
    kernel = jnp.exp((cosine - 1.0) / 0.05)
    total_rows = passages.shape[0] * lax.axis_size("rows")
    total_cents = centroids.shape[0] * lax.axis_size("cent")
    ratio = jnp.float32(total_rows) / jnp.float32(total_cents)
    row_scale = jnp.ones((passages.shape[0],), jnp.float32)
    for step in range(ITERS):
        col_local = jnp.dot(row_scale, kernel, precision=lax.Precision.HIGHEST)
        col_total = lax.psum(col_local, "rows")
        col_scale = ratio / col_total
        row_local = jnp.dot(kernel, col_scale, precision=lax.Precision.HIGHEST)
        row_total = lax.psum(row_local, "cent")
        row_scale = 1.0 / row_total
    plan = (row_scale[:, None] * kernel).astype(jnp.bfloat16)
    terms = lax.dot_general(
        plan, unit_rows, (((0,), (0,)), ((), ())), preferred_element_type=jnp.float32
    )
    sums = lax.psum(terms, "rows")
    new_centroids = sums * lax.rsqrt(jnp.mean(sums * sums, axis=-1, keepdims=True) + 1e-06)
    return (new_centroids, jnp.log(row_scale))


def solution(mesh):
    placed = (P("rows", None), P("cent", None))
    return jax.shard_map(
        shards, mesh=mesh, in_specs=placed, out_specs=(P("cent", None), P("rows")), check_vma=False
    )
```

profile of v0, /device:TPU:0, one launch (start us, length us, event | category | flops | bytes accessed | tf_op | source)
XLA Modules:
  0.0 992.1 jit_solution(9778771079682798152)
XLA Ops:
  7.2 0.0 all-reduce.2.cloned.1.call-start
  7.2 4.1 fusion.4
  11.3 4.1 fusion.2
  15.4 41.3 %multiply_exponential_fusion = f32[4096,4096]{1,0:T(8,128)} fusion(bf16[4096,768]{1,0:T(8,128)(2,1)} %param.3, f32[4096]{0:T(1024)S(1)} %get-tuple-element.4, bf16[4096,768]{1,0:T(8,128)(2,1)} %param.2, f32[4096]{0:T(1024)S(1)} %get-tuple-element.5), kind=kOutput, calls=%fused_computation.1 | convolution fusion | flops 25839009792 | bytes 79724544 | tf_op jit(solution)/shard_map/dot_general | solution.py:18
  56.7 36.1 %fusion.10 = f32[1,4096]{1,0:T(1,128)S(1)} fusion(f32[4096,4096]{1,0:T(8,128)} %multiply_exponential_fusion), kind=kOutput, calls=%fused_computation.18 | convolution fusion | flops 201326592 | bytes 67125248 | tf_op jit(solution)/shard_map/dot_general | solution.py:25
  92.7 78.5 %psum.49 = f32[4096]{0:T(1024)S(1)} all-reduce(f32[4096]{0:T(1024)S(1)} %bitcast.32), channel_id=1, replica_groups=mesh['rows'=16,'cent'=2] {'rows'}, use_global_device_ids=true, to_apply=%region_2.0 | all-reduce | flops 4096 | bytes 32768 | tf_op jit(solution)/shard_map/psum | solution.py:26
  171.3 59.9 %fusion.14 = f32[1,4096]{1,0:T(1,128)S(1)} fusion(f32[4096,4096]{1,0:T(8,128)} %multiply_exponential_fusion, f32[4096,1]{0,1:T(1,128)S(1)} %bitcast.27), kind=kOutput, calls=%fused_computation.28 | convolution fusion | flops 201326592 | bytes 67141632 | tf_op jit(solution)/shard_map/dot_general | solution.py:28
  231.2 3.4 psum.50
  234.5 35.8 %fusion.15 = f32[1,4096]{1,0:T(1,128)S(1)} fusion(f32[4096,1]{0,1:T(1,128)S(1)} %bitcast.22, f32[4096,4096]{1,0:T(8,128)} %multiply_exponential_fusion), kind=kOutput, calls=%fused_computation.29 | convolution fusion | flops 201326592 | bytes 67141632 | tf_op jit(solution)/shard_map/dot_general | solution.py:25
  270.3 71.7 %psum.51 = f32[4096]{0:T(1024)S(1)} all-reduce(f32[4096]{0:T(1024)S(1)} %bitcast.28), channel_id=1, replica_groups=mesh['rows'=16,'cent'=2] {'rows'}, use_global_device_ids=true, to_apply=%region_4.0 | all-reduce | flops 4096 | bytes 32768 | tf_op jit(solution)/shard_map/psum | solution.py:26
  342.1 59.9 %fusion.16 = f32[1,4096]{1,0:T(1,128)S(1)} fusion(f32[4096,4096]{1,0:T(8,128)} %multiply_exponential_fusion, f32[4096,1]{0,1:T(1,128)S(1)} %bitcast.29), kind=kOutput, calls=%fused_computation.30 | convolution fusion | flops 201326592 | bytes 67141632 | tf_op jit(solution)/shard_map/dot_general | solution.py:28
  402.0 3.4 psum.52
  405.3 35.9 %fusion.17 = f32[1,4096]{1,0:T(1,128)S(1)} fusion(f32[4096,1]{0,1:T(1,128)S(1)} %bitcast.23, f32[4096,4096]{1,0:T(8,128)} %multiply_exponential_fusion), kind=kOutput, calls=%fused_computation.31 | convolution fusion | flops 201326592 | bytes 67141632 | tf_op jit(solution)/shard_map/dot_general | solution.py:25
  441.2 71.7 %psum.53 = f32[4096]{0:T(1024)S(1)} all-reduce(f32[4096]{0:T(1024)S(1)} %bitcast.30), channel_id=1, replica_groups=mesh['rows'=16,'cent'=2] {'rows'}, use_global_device_ids=true, to_apply=%region_6.0 | all-reduce | flops 4096 | bytes 32768 | tf_op jit(solution)/shard_map/psum | solution.py:26
  512.9 59.9 %fusion.18 = f32[1,4096]{1,0:T(1,128)S(1)} fusion(f32[4096,4096]{1,0:T(8,128)} %multiply_exponential_fusion, f32[4096,1]{0,1:T(1,128)S(1)} %bitcast.31), kind=kOutput, calls=%fused_computation.32 | convolution fusion | flops 201326592 | bytes 67141632 | tf_op jit(solution)/shard_map/dot_general | solution.py:28
  572.8 3.4 psum.54
  576.2 0.6 fusion.13
  576.8 38.9 %fusion = f32[4096,768]{1,0:T(8,128)} fusion(f32[4096,4096]{1,0:T(8,128)} %multiply_exponential_fusion, f32[4096]{0:T(1024)S(1)} %get-tuple-element.3, bf16[4096,768]{1,0:T(8,128)(2,1)} %param.2, f32[4096]{0:T(1024)S(1)} %get-tuple-element.5), kind=kOutput, calls=%fused_computation.2 | convolution fusion | flops 25812795392 | bytes 86016000 | tf_op jit(solution)/shard_map/dot_general | solution.py:32
  615.7 0.0 all-reduce.2.cloned.1.call-update
  615.8 353.3 %all-reduce.2.cloned.1.call-done = f32[4096,768]{1,0:T(8,128)} async-done(((f32[4096,768]{1,0:T(8,128)}), f32[4096,768]{1,0:T(8,128)}) %all-reduce.2.cloned.1.call-update) | async-done | bytes 12582928 | tf_op jit(solution)/shard_map/psum | solution.py:35
  969.1 5.5 multiply_reduce_fusion
  974.6 10.2 %broadcast_multiply_fusion = f32[4096,768]{1,0:T(8,128)} fusion(f32[4096,768]{1,0:T(8,128)} %all-reduce.2.cloned.1.call-done, f32[4096]{0:T(1024)S(1)} %add_rsqrt_fusion), kind=kLoop, calls=%fused_computation.13 | loop fusion | flops 3145728 | bytes 25182208 | tf_op jit(solution)/shard_map/mul | solution.py:36
  (7 shorter events, 0.1 us)
Async XLA Ops:
  7.2 961.9 %all-reduce.2.cloned.1.call-start = ((), (), s32[]{:S(2)}) async-start(), calls=%async_computation | async-start | bytes 25165824 | tf_op jit(solution)/shard_map/psum | solution.py:35
Sparse Core Ops, SparseCore 0:
  615.9 353.1 all-reduce.1
where the time goes:
time: 1000 us; the launch traced here: 992 us
  matrix products  368 us (37%)
  waiting for transfers between devices  353 us (35%)
  blocking collectives  232 us (23%)
  other arithmetic  24.6 us (2%)
  between operations  14.5 us (1%)
    psum x1, waiting for transfers between devices, shards(): sums = lax.psum(terms, 'rows')  353 us
    psum x3, blocking collectives, shards(): col_total = lax.psum(col_local, 'rows')  222 us
    dot_general x3, matrix products, shards(): row_local = jnp.dot(kernel, col_scale, precision=lax.Precision.HIGHEST)  180 us
    dot_general x3, matrix products, shards(): col_local = jnp.dot(row_scale, kernel, precision=lax.Precision.HIGHEST)  108 us
    dot_general x1, matrix products, shards(): jnp.dot(unit_rows, unit_cents.T, preferred_element_type=jnp.float32) / width  41.3 us
    dot_general x1, matrix products, shards(): lax.dot_general(plan, unit_rows, (((0,), (0,)), ((), ())), preferred_elem...  38.9 us
  transfers between devices with their start and end apart: 1, of which 1 were waited for; matrix products, arithmetic and copies ran while one was open for 0% of the time, Pallas kernels for 0%

commit v1 on v0

v1 whole, which is shorter than its diff:
```python
import functools
import math

import jax
import jax.numpy as jnp
from jax import lax
from jax.experimental import pallas as pl
from jax.experimental.pallas import tpu as pltpu
from jax.sharding import PartitionSpec as P

ITERS = 3
MESH = pl.DeviceIdType.MESH
F32 = jnp.float32
BF16 = jnp.bfloat16
CENT_BLOCK = 256
ROW_BLOCK = 1024
PASS_BLOCK = 512


def unit_scale(values):
    full = values.astype(F32)
    return full * lax.rsqrt(jnp.mean(full * full, axis=-1, keepdims=True) + 1e-06)


def split_rows(vector):
    high = vector.astype(BF16).astype(F32)
    low = vector - high
    which = lax.broadcasted_iota(jnp.int32, (16, vector.shape[1]), 0)
    return jnp.where(which == 0, high, jnp.where(which == 1, low, 0.0)).astype(BF16)


def blocks(size, block, body):
    block = min(size, block)

    def step(index, carry):
        body(pl.ds(pl.multiple_of(index * block, block), block), block, index)
        return carry

    lax.fori_loop(0, size // block, step, 0)


def sinkhorn_kernel(
    n_rows, n_cent, ratio,
    rows_hbm, cents_hbm, sums_hbm, log_ref,
    kern, unit, cents, out_buf, col_vec, row_vec, row_scale,
    col_slots, row_slots, in_sem, out_sem, col_send, col_recv, row_send, row_recv,
):
    rows, width = unit.shape
    n_local = cents.shape[0]
    me_row = lax.axis_index("rows")
    me_cent = lax.axis_index("cent")
    part = rows // 4
    loads = [
        pltpu.make_async_copy(
            rows_hbm.at[pl.ds(q * part, part)], unit.at[pl.ds(q * part, part)], in_sem.at[q]
        )
        for q in range(4)
    ]
    loads.append(pltpu.make_async_copy(cents_hbm, cents, in_sem.at[4]))
    for load in loads:
        load.start()

    barrier = pltpu.get_barrier_semaphore()
    for off in range(1, n_rows):
        pl.semaphore_signal(
            barrier, inc=1, device_id={"rows": lax.rem(me_row + off, n_rows)}, device_id_type=MESH
        )
    for off in range(1, n_cent):
        pl.semaphore_signal(
            barrier, inc=1, device_id={"cent": lax.rem(me_cent + off, n_cent)}, device_id_type=MESH
        )

    for q in range(4):
        loads[q].wait()

        def normalize(where, block, index, q=q):
            at = pl.ds(pl.multiple_of(q * part + index * block, block), block)
            unit[at, :] = unit_scale(unit[at, :]).astype(BF16)

        blocks(part, 256, normalize)
    loads[4].wait()

    slope = 20.0 * math.log2(math.e) / width
    offset = 20.0 * math.log2(math.e)
    row_block = min(rows, ROW_BLOCK)

    def make_kernel(where, block, index):
        unit_cents = unit_scale(cents[where, :]).astype(BF16)
        acc = jnp.zeros((block, 128), F32)
        for b in range(rows // row_block):
            here = slice(b * row_block, (b + 1) * row_block)
            dot = lax.dot_general(
                unit_cents, unit[here, :], (((1,), (1,)), ((), ())), preferred_element_type=F32
            )
            value = jnp.exp2(dot * slope - offset)
            kern[where, here] = value.astype(BF16)
            for lane in range(row_block // 128):
                acc = acc + value[:, lane * 128:(lane + 1) * 128]
        col_slots[0, 0, :, where] = jnp.sum(acc.T, axis=0, keepdims=True)

    blocks(n_local, CENT_BLOCK, make_kernel)
    pl.semaphore_wait(barrier, n_rows - 1 + n_cent - 1)

    for t in range(ITERS):
        copies = []
        for off in range(1, n_rows):
            copies.append(pltpu.make_async_remote_copy(
                src_ref=col_slots.at[t, 0],
                dst_ref=col_slots.at[t, off],
                send_sem=col_send.at[t, off],
                recv_sem=col_recv.at[t, off],
                device_id={"rows": lax.rem(me_row + off, n_rows)},
                device_id_type=MESH,
            ))
        for copy in copies:
            copy.start()
        for copy in copies:
            copy.wait()
        total = col_slots[t, 0]
        for off in range(1, n_rows):
            total = total + col_slots[t, off]
        col_vec[...] = split_rows(ratio / total)

        def row_pass(where, block, index):
            mass = jnp.dot(col_vec[...], kern[:, where], preferred_element_type=F32)
            row_slots[t, me_cent, :, where] = jnp.sum(mass, axis=0, keepdims=True)

        blocks(rows, PASS_BLOCK, row_pass)
        copies = []
        for off in range(1, n_cent):
            copies.append(pltpu.make_async_remote_copy(
                src_ref=row_slots.at[t, me_cent],
                dst_ref=row_slots.at[t, me_cent],
                send_sem=row_send.at[t, off],
                recv_sem=row_recv.at[t, off],
                device_id={"cent": lax.rem(me_cent + off, n_cent)},
                device_id_type=MESH,
            ))
        for copy in copies:
            copy.start()
        for copy in copies:
            copy.wait()
        total = row_slots[t, 0]
        for other in range(1, n_cent):
            total = total + row_slots[t, other]
        scale = 1.0 / total
        if t < ITERS - 1:
            row_vec[...] = split_rows(scale)

            def col_pass(where, block, index):
                mass = lax.dot_general(
                    row_vec[...], kern[where, :], (((1,), (1,)), ((), ())),
                    preferred_element_type=F32,
                )
                col_slots[t + 1, 0, :, where] = jnp.sum(mass, axis=0, keepdims=True)

            blocks(n_local, PASS_BLOCK, col_pass)
        else:
            row_scale[...] = scale
            log_ref[...] = jnp.log(scale)

    out_block = min(CENT_BLOCK, n_local)
    steps = n_local // out_block

    def store(index, slot):
        at = pl.ds(pl.multiple_of(index * out_block, out_block), out_block)
        return pltpu.make_async_copy(out_buf.at[slot], sums_hbm.at[at], out_sem.at[slot])

    def weigh(index, carry):
        slot = lax.rem(index, 2)
        at = pl.ds(pl.multiple_of(index * out_block, out_block), out_block)

        @pl.when(index >= 2)
        def _():
            store(index - 2, slot).wait()

        total = jnp.zeros((out_block, width), F32)
        for b in range(rows // row_block):
            here = slice(b * row_block, (b + 1) * row_block)
            plan = (kern[at, here].astype(F32) * row_scale[:, here]).astype(BF16)
            total = total + jnp.dot(plan, unit[here, :], preferred_element_type=F32)
        out_buf[slot] = total
        store(index, slot).start()
        return carry

    lax.fori_loop(0, steps, weigh, 0)
    for index in range(max(steps - 2, 0), steps):
        store(index, index % 2).wait()


def balance(passages, centroids, n_rows, n_cent):
    rows, width = passages.shape
    n_local = centroids.shape[0]
    ratio = float(rows * n_rows) / float(n_local * n_cent)
    dma = pltpu.SemaphoreType.DMA
    return pl.pallas_call(
        functools.partial(sinkhorn_kernel, n_rows, n_cent, ratio),
        out_shape=(
            jax.ShapeDtypeStruct((n_local, width), F32),
            jax.ShapeDtypeStruct((1, rows), F32),
        ),
        in_specs=[pl.BlockSpec(memory_space=pl.ANY)] * 2,
        out_specs=(pl.BlockSpec(memory_space=pl.ANY), pl.BlockSpec(memory_space=pltpu.VMEM)),
        scratch_shapes=[
            pltpu.VMEM((n_local, rows), BF16),
            pltpu.VMEM((rows, width), BF16),
            pltpu.VMEM((n_local, width), BF16),
            pltpu.VMEM((2, min(CENT_BLOCK, n_local), width), F32),
            pltpu.VMEM((16, n_local), BF16),
            pltpu.VMEM((16, rows), BF16),
            pltpu.VMEM((1, rows), F32),
            pltpu.VMEM((ITERS, n_rows, 1, n_local), F32),
            pltpu.VMEM((ITERS, n_cent, 1, rows), F32),
            dma((5,)), dma((2,)),
            dma((ITERS, n_rows)), dma((ITERS, n_rows)),
            dma((ITERS, n_cent)), dma((ITERS, n_cent)),
        ],
        compiler_params=pltpu.CompilerParams(
            collective_id=0, has_side_effects=True, vmem_limit_bytes=60 * 1024 * 1024
        ),
        name="balance",
    )(passages, centroids)


def shards(n_rows, n_cent, passages, centroids):
    terms, logs = balance(passages, centroids, n_rows, n_cent)
    sums = lax.psum(terms, "rows")
    new_centroids = sums * lax.rsqrt(jnp.mean(sums * sums, axis=-1, keepdims=True) + 1e-06)
    return (new_centroids, logs.reshape(-1))


def solution(mesh):
    placed = (P("rows", None), P("cent", None))
    return jax.shard_map(
        functools.partial(shards, mesh.shape["rows"], mesh.shape["cent"]),
        mesh=mesh, in_specs=placed, out_specs=(P("cent", None), P("rows")), check_vma=False,
    )
```

time: 1000 us -> 521 us (0.52)
  matrix products: 368 us -> 0 us
  blocking collectives: 232 us -> 0 us
  Pallas kernels: 0 us -> 132 us
    dot_general x8 -> x0, matrix products: 368 us -> none  [the longest x3 180 us: shards(): row_local = jnp.dot(kernel, col_scale, precision=lax.Precision.HIGHEST)]
    psum x6 -> x0, blocking collectives: 232 us -> none  [the longest x3 222 us: shards(): col_total = lax.psum(col_local, 'rows')]
    pallas_call x0 -> x1, Pallas kernels: none -> 132 us  [balance(): pl.pallas_call(functools.partial(sinkhorn_kernel, n_rows, n_cent, ratio),...]
where the time goes in v1:
time: 521 us
  waiting for transfers between devices  359 us (69%)
  Pallas kernels  132 us (25%)
  other arithmetic  15.7 us (3%)
  between operations  14.1 us (3%)
    psum x1, waiting for transfers between devices, shards(): sums = lax.psum(terms, 'rows')  359 us
    pallas_call x1, Pallas kernels, balance(): pl.pallas_call(functools.partial(sinkhorn_kernel, n_rows, n_cent, ratio),...  132 us
  transfers between devices with their start and end apart: 1, of which 1 were waited for; matrix products, arithmetic and copies ran while one was open for 0% of the time, Pallas kernels for 0%

profile of v1, /device:TPU:0, one launch (start us, length us, event | category | flops | bytes accessed | tf_op | source)
XLA Modules:
  0.0 520.8 jit_solution(9184141800290513796)
XLA Ops:
  7.2 0.0 all-reduce.2.cloned.1.call-start
  7.2 131.8 %balance.1 = (f32[4096,768]{1,0:T(8,128)}, f32[1,4096]{1,0:T(1,128)}) custom-call(bf16[4096,768]{1,0:T(8,128)(2,1)} %rows_hbm.1, bf16[4096,768]{1,0:T(8,128)(2,1)} %cents_hbm.1), custom_call_target="tpu_custom_call" | custom-call | tf_op jit(solution)/shard_map/balance/pallas_call | solution.py:196
  139.0 0.0 all-reduce.2.cloned.1.call-update
  139.0 358.6 %all-reduce.2.cloned.1.call-done = f32[4096,768]{1,0:T(8,128)} async-done(((f32[4096,768]{1,0:T(8,128)}), f32[4096,768]{1,0:T(8,128)}) %all-reduce.2.cloned.1.call-update) | async-done | bytes 12582928 | tf_op jit(solution)/shard_map/psum | solution.py:227
  497.6 5.5 %multiply_reduce_fusion = f32[4096]{0:T(1024)S(1)} fusion(f32[4096,768]{1,0:T(8,128)} %all-reduce.2.cloned.1.call-done), kind=kLoop, calls=%fused_computation | loop fusion | flops 6287360 | bytes 12599296 | tf_op jit(solution)/shard_map/reduce_sum | solution.py:228
  503.1 0.0 copy-start
  503.1 10.2 %broadcast_multiply_fusion = f32[4096,768]{1,0:T(8,128)} fusion(f32[4096,768]{1,0:T(8,128)} %all-reduce.2.cloned.1.call-done, f32[4096]{0:T(1024)S(1)} %add_rsqrt_fusion), kind=kLoop, calls=%fused_computation.1 | loop fusion | flops 3145728 | bytes 25182208 | tf_op jit(solution)/shard_map/mul | solution.py:228
  513.3 0.0 copy-done
  513.3 0.6 copy.6
  (1 shorter events, 0.0 us)
Async XLA Ops:
  7.2 490.4 %all-reduce.2.cloned.1.call-start = ((), (), s32[]{:S(2)}) async-start(), calls=%async_computation | async-start | bytes 25165824 | tf_op jit(solution)/shard_map/psum | solution.py:227
  503.1 10.2 %copy-start = (f32[1,4096]{1,0:T(1,128)S(1)}, f32[1,4096]{1,0:T(1,128)}, u32[]{:S(2)}) copy-start(f32[1,4096]{1,0:T(1,128)} %get-tuple-element.5) | copy-start | bytes 49156
Sparse Core Ops, SparseCore 0:
  139.1 358.4 all-reduce.1

commit v2 on v1

--- a/solution.py
+++ b/solution.py
@@ -15,6 +15,7 @@
 CENT_BLOCK = 256
 ROW_BLOCK = 1024
 PASS_BLOCK = 512
+PIECES = 4
 
 
 def unit_scale(values):
@@ -222,11 +223,162 @@
     )(passages, centroids)
 
 
+def reduce_kernel(grid, streams, width, terms_hbm, out_hbm, total, *scratch):
+    count = len(streams)
+    landing = [scratch[3 * i:3 * i + 3] for i in range(count)]
+    load_sem, own_sem, send_sem, recv_sem = scratch[3 * count:]
+    me = lax.axis_index("rows")
+    sizes = dict(zip("zyx", grid))
+    strides = {"z": grid[1] * grid[2], "y": grid[2], "x": 1}
+    at = {axis: lax.rem(lax.div(me, strides[axis]), sizes[axis]) for axis in "zyx"}
+
+    def neighbour(axis, off):
+        value = lax.rem(at[axis] + off, sizes[axis])
+        return value, {"rows": me + (value - at[axis]) * strides[axis]}
+
+    def load(i, p):
+        order, start, rows, pieces = streams[i]
+        where = pl.ds(start + p * rows, rows)
+        return pltpu.make_async_copy(terms_hbm.at[where], total.at[where], load_sem.at[i, p])
+
+    most = max(stream[3] for stream in streams)
+    for p in range(most):
+        for i in range(count):
+            if p < streams[i][3]:
+                load(i, p).start()
+
+    barrier = pltpu.get_barrier_semaphore()
+    for axis in "zyx":
+        for off in range(1, sizes[axis]):
+            pl.semaphore_signal(
+                barrier, inc=1, device_id=neighbour(axis, off)[1], device_id_type=MESH
+            )
+    pl.semaphore_wait(barrier, sum(grid) - 3)
+
+    def share(i, p, level, value):
+        order, start, rows, pieces = streams[i]
+        first, height = start + p * rows, rows
+        for k in range(level + 1):
+            height = height // sizes[order[k]]
+            first = first + (value if k == level else at[order[k]]) * height
+        return pl.ds(pl.multiple_of(first, 8), height)
+
+    def reduces(i, p, level):
+        axis = streams[i][0][level]
+        copies = []
+        for off in range(1, sizes[axis]):
+            value, device = neighbour(axis, off)
+            copies.append(pltpu.make_async_remote_copy(
+                src_ref=total.at[share(i, p, level, value)],
+                dst_ref=landing[i][level].at[p, off - 1],
+                send_sem=send_sem.at[i, level, p, off - 1],
+                recv_sem=recv_sem.at[i, level, p, off - 1],
+                device_id=device, device_id_type=MESH,
+            ))
+        return copies
+
+    def gathers(i, p, level):
+        axis = streams[i][0][level]
+        block = share(i, p, level, at[axis])
+        source = total if level == 2 else out_hbm
+        copies = []
+        for off in range(1, sizes[axis]):
+            copies.append(pltpu.make_async_remote_copy(
+                src_ref=source.at[block], dst_ref=out_hbm.at[block],
+                send_sem=send_sem.at[i, 5 - level, p, off - 1],
+                recv_sem=recv_sem.at[i, 5 - level, p, off - 1],
+                device_id=neighbour(axis, off)[1], device_id_type=MESH,
+            ))
+        return copies
+
+    def own(i, p):
+        block = share(i, p, 2, at[streams[i][0][2]])
+        return pltpu.make_async_copy(total.at[block], out_hbm.at[block], own_sem.at[i, p])
+
+    def accumulate(i, p, level):
+        axis = streams[i][0][level]
+        block = share(i, p, level, at[axis])
+        height = block.size
+        step = math.gcd(height, 32)
+
+        def add(index, carry):
+            here = pl.ds(pl.multiple_of(index * step, 8), step)
+            there = pl.ds(pl.multiple_of(block.start + index * step, 8), step)
+            value = total[there, :]
+            for off in range(1, sizes[axis]):
+                value = value + landing[i][level][p, off - 1, here, :]
+            if level == 2:
+                value = value * lax.rsqrt(jnp.mean(value * value, axis=-1, keepdims=True) + 1e-06)
+            total[there, :] = value
+            return carry
+
+        lax.fori_loop(0, height // step, add, 0)
+
+    def stage(i, p, number):
+        if number == 0:
+            load(i, p).wait()
+        elif number <= 3:
+            for copy in reduces(i, p, number - 1):
+                copy.wait()
+            accumulate(i, p, number - 1)
+        else:
+            for copy in gathers(i, p, 6 - number):
+                copy.wait()
+            if number == 4:
+                own(i, p).wait()
+        if number < 3:
+            begin = reduces(i, p, number)
+        elif number < 6:
+            begin = gathers(i, p, 5 - number)
+        else:
+            begin = []
+        for copy in begin:
+            copy.start()
+        if number == 3:
+            own(i, p).start()
+
+    for slot in range(most + 6):
+        for number in range(7):
+            for i in range(count):
+                if 0 <= slot - number < streams[i][3]:
+                    stage(i, slot - number, number)
+
+
+def reduce_all(terms, n_rows):
+    height, width = terms.shape
+    grid = {16: (4, 2, 2), 32: (2, 4, 4)}.get(n_rows, (n_rows, 1, 1))
+    half = height // 2
+    pieces = max(1, min(PIECES, half // (8 * n_rows)))
+    streams = (("xyz", 0, half // pieces, pieces), ("yxz", half, half // pieces, pieces))
+    sizes = dict(zip("zyx", grid))
+    landing = []
+    for order, start, rows, count in streams:
+        for axis in order:
+            rows = rows // sizes[axis]
+            landing.append(pltpu.VMEM((count, max(1, sizes[axis] - 1), rows, width), F32))
+    dma = pltpu.SemaphoreType.DMA
+    most = max(stream[3] for stream in streams)
+    flags = dma((len(streams), 6, most, max(1, max(grid) - 1)))
+    return pl.pallas_call(
+        functools.partial(reduce_kernel, grid, streams, width),
+        out_shape=jax.ShapeDtypeStruct((height, width), F32),
+        in_specs=[pl.BlockSpec(memory_space=pl.ANY)],
+        out_specs=pl.BlockSpec(memory_space=pl.ANY),
+        scratch_shapes=[
+            pltpu.VMEM((height, width), F32),
+            *landing,
+            dma((len(streams), most)), dma((len(streams), most)), flags, flags,
+        ],
+        compiler_params=pltpu.CompilerParams(
+            collective_id=1, has_side_effects=True, vmem_limit_bytes=48 * 1024 * 1024
+        ),
+        name="reduce_all",
+    )(terms)
+
+
 def shards(n_rows, n_cent, passages, centroids):
     terms, logs = balance(passages, centroids, n_rows, n_cent)
-    sums = lax.psum(terms, "rows")
-    new_centroids = sums * lax.rsqrt(jnp.mean(sums * sums, axis=-1, keepdims=True) + 1e-06)
-    return (new_centroids, logs.reshape(-1))
+    return (reduce_all(terms, n_rows), logs.reshape(-1))
 
 
 def solution(mesh):

time: 521 us -> 398 us (0.76)
  waiting for transfers between devices: 359 us -> 0 us
  Pallas kernels: 132 us -> 386 us
  other arithmetic: 15.7 us -> 0 us
  between operations: 14.1 us -> 0.65 us
  local copies, waits for them, and re-layouts: 0.61 us -> 10.8 us
    psum x1 -> x0, waiting for transfers between devices: 359 us -> none  [shards(): sums = lax.psum(terms, 'rows')]
    pallas_call x0 -> x1, Pallas kernels: none -> 255 us  [reduce_all(): pl.pallas_call(functools.partial(reduce_kernel, grid, streams, width), ou...]
    mul x1 -> x0, other arithmetic: 10.2 us -> none  [shards(): sums * lax.rsqrt(jnp.mean(sums * sums, axis=-1, keepdims=True) + 1e-06)]
    unnamed x3 -> x4, local copies, waits for them, and re-layouts: 0.61 us -> 10.8 us
    reduce_sum x1 -> x0, other arithmetic: 5.47 us -> none  [shards(): jnp.mean(sums * sums, axis=-1, keepdims=True) + 1e-06]
  transfers between devices with their start and end apart: 1 -> 0, of which waited for: 1 -> 0; matrix products, arithmetic and copies ran while one was open for 0% -> 0% of each run, Pallas kernels for 0% -> 0%
where the time goes in v2:
time: 398 us
  Pallas kernels  386 us (97%)
  local copies, waits for them, and re-layouts  10.8 us (3%)
    pallas_call x1, Pallas kernels, reduce_all(): pl.pallas_call(functools.partial(reduce_kernel, grid, streams, width), ou...  255 us
    pallas_call x1, Pallas kernels, balance(): pl.pallas_call(functools.partial(sinkhorn_kernel, n_rows, n_cent, ratio),...  132 us
    unnamed x4, local copies, waits for them, and re-layouts  10.8 us

profile of v2, /device:TPU:0, one launch (start us, length us, event | category | flops | bytes accessed | tf_op | source)
XLA Modules:
  0.0 397.8 jit_solution(13774455710306830112)
XLA Ops:
  0.6 131.8 %balance.1 = (f32[4096,768]{1,0:T(8,128)}, f32[1,4096]{1,0:T(1,128)}) custom-call(bf16[4096,768]{1,0:T(8,128)(2,1)} %rows_hbm.1, bf16[4096,768]{1,0:T(8,128)(2,1)} %cents_hbm.1), custom_call_target="tpu_custom_call" | custom-call | tf_op jit(solution)/shard_map/balance/pallas_call | solution.py:197
  132.4 254.6 %reduce_all.1 = f32[4096,768]{1,0:T(8,128)} custom-call(f32[4096,768]{1,0:T(8,128)} %get-tuple-element.4.terms_hbm), custom_call_target="tpu_custom_call" | custom-call | tf_op jit(solution)/shard_map/reduce_all/pallas_call | solution.py:362
  387.0 0.0 copy-start
  387.0 10.2 %copy.6 = f32[4096,768]{1,0:T(8,128)} copy(f32[4096,768]{1,0:T(8,128)} %reduce_all.1) | data formatting | bytes 25165824
  397.2 0.0 copy-done
  397.2 0.6 copy.7
Async XLA Ops:
  387.0 10.2 %copy-start = (f32[1,4096]{1,0:T(1,128)S(1)}, f32[1,4096]{1,0:T(1,128)}, u32[]{:S(2)}) copy-start(f32[1,4096]{1,0:T(1,128)} %get-tuple-element.5) | copy-start | bytes 49156

commit v3 on v2

--- a/solution.py
+++ b/solution.py
@@ -15,7 +15,7 @@
 CENT_BLOCK = 256
 ROW_BLOCK = 1024
 PASS_BLOCK = 512
-PIECES = 4
+SHARES = (("xyz", 2, 8), ("yxz", 2, 8))
 
 
 def unit_scale(values):
@@ -344,12 +344,16 @@
                     stage(i, slot - number, number)
 
 
-def reduce_all(terms, n_rows):
+def reduce_all(terms, n_rows, shares=SHARES):
     height, width = terms.shape
     grid = {16: (4, 2, 2), 32: (2, 4, 4)}.get(n_rows, (n_rows, 1, 1))
-    half = height // 2
-    pieces = max(1, min(PIECES, half // (8 * n_rows)))
-    streams = (("xyz", 0, half // pieces, pieces), ("yxz", half, half // pieces, pieces))
+    if height * 2 // 32 % (8 * n_rows):
+        shares = (("xyz", 1, 1), ("yxz", 1, 1))
+    unit = height // sum(rows * pieces for order, rows, pieces in shares)
+    streams, start = [], 0
+    for order, rows, pieces in shares:
+        streams.append((order, start, rows * unit, pieces))
+        start += rows * unit * pieces
     sizes = dict(zip("zyx", grid))
     landing = []
     for order, start, rows, count in streams:

time: 398 us -> 358 us (0.90)
  Pallas kernels: 386 us -> 346 us
    pallas_call x1, Pallas kernels: 255 us -> 214 us  [reduce_all(): pl.pallas_call(functools.partial(reduce_kernel, grid, streams, width), ou...]
where the time goes in v3:
time: 358 us; the launch traced here: 357 us
  Pallas kernels  346 us (97%)
  local copies, waits for them, and re-layouts  10.8 us (3%)
    pallas_call x1, Pallas kernels, reduce_all(): pl.pallas_call(functools.partial(reduce_kernel, grid, streams, width), ou...  214 us
    pallas_call x1, Pallas kernels, balance(): pl.pallas_call(functools.partial(sinkhorn_kernel, n_rows, n_cent, ratio),...  132 us
    unnamed x4, local copies, waits for them, and re-layouts  10.8 us

profile of v3, /device:TPU:0, one launch (start us, length us, event | category | flops | bytes accessed | tf_op | source)
XLA Modules:
  0.0 357.4 jit_solution(8731272741027357366)
XLA Ops:
  0.6 131.8 %balance.1 = (f32[4096,768]{1,0:T(8,128)}, f32[1,4096]{1,0:T(1,128)}) custom-call(bf16[4096,768]{1,0:T(8,128)(2,1)} %rows_hbm.1, bf16[4096,768]{1,0:T(8,128)(2,1)} %cents_hbm.1), custom_call_target="tpu_custom_call" | custom-call | tf_op jit(solution)/shard_map/balance/pallas_call | solution.py:197
  132.4 214.2 %reduce_all.1 = f32[4096,768]{1,0:T(8,128)} custom-call(f32[4096,768]{1,0:T(8,128)} %get-tuple-element.4.terms_hbm), custom_call_target="tpu_custom_call" | custom-call | tf_op jit(solution)/shard_map/reduce_all/pallas_call | solution.py:366
  346.6 0.0 copy-start
  346.7 10.2 %copy.6 = f32[4096,768]{1,0:T(8,128)} copy(f32[4096,768]{1,0:T(8,128)} %reduce_all.1) | data formatting | bytes 25165824
  356.8 0.0 copy-done
  356.8 0.6 copy.7
Async XLA Ops:
  346.6 10.2 %copy-start = (f32[1,4096]{1,0:T(1,128)S(1)}, f32[1,4096]{1,0:T(1,128)}, u32[]{:S(2)}) copy-start(f32[1,4096]{1,0:T(1,128)} %get-tuple-element.5) | copy-start | bytes 49156
